TPU v7x, 128 devices: a whole 4x4x4 slice. The times are simulated.
128 devices in a mesh: blk: 16 (over y, z), beam: 8 (over x, core).
Axes of the slice: x: 4, y: 4, z: 4, core: 2. Of those that a mesh axis runs over, the one named last changes fastest.
Arguments:
- signal: float32 [2097152], P(('blk', 'beam')), may hold values from -6 to 6
- weight: float32 [2097152], P(('blk', 'beam')), may hold values from 0.25 to 1
- cycle: int32 [2097152], P(('blk', 'beam')), may hold values from 0 to 1
- phi: int32 [2097152], P(('blk', 'beam')), may hold values from 0 to 2047
- psi: int32 [2097152], P(('blk', 'beam')), may hold values from 0 to 31
- owner: int32 [16384, 1], P(('blk', 'beam')), may hold values from 0 to 15; in each aligned block of 128 rows (0 to 127, 128 to 255, ...) at most 20 rows name the same one
- wigner: bfloat16 [1024, 32, 32, 1152], P('blk', 'beam'), may hold values from -0.25 to 0.25
Outputs:
- alm: float32 [1024, 2, 1152], P(('blk', 'beam'))
Inputs may be any that keep to these rules, and one draw needn't show every extreme that they name: `owner`: among the 128 blocks of one device no cycle group is named by more than 20 blocks, and in some device's blocks one group is named by exactly 20.
All inputs are finite; a program needn't handle non-finite values.
Results may differ from a plain program's by a relative error of at most 0.02.
Values may be sent and summed in bfloat16 or wider, within the bound.
A program may use at most 128 MiB of HBM per device.

v0:
```python
import math

import jax
import jax.numpy as jnp
from jax import lax
from jax.sharding import PartitionSpec as P

BLOCK_ROWS = 128
CYCLE_DEV = 2
NPSI = 32
NPHI = 2048


def psi_rows(psi_index, length):
    component = jnp.arange(length, dtype=jnp.int32)[:, None]
    middle = length // 2
    frequency = jnp.where(component <= middle, component, component - middle)
    residue = (frequency * psi_index[None, :] % length).astype(jnp.float32)
    angles = residue * jnp.float32(2.0 * math.pi / length)
    return jnp.where(component <= middle, jnp.cos(angles), jnp.sin(angles)) * jnp.float32(
        1.0 / math.sqrt(length)
    )


def phi_table(length):
    cell_index = jnp.arange(length, dtype=jnp.int32)[:, None]
    column = jnp.arange(length, dtype=jnp.int32)[None, :]
    residue = (column // 2 * cell_index % length).astype(jnp.float32)
    angles = residue * jnp.float32(2.0 * math.pi / length)
    values = jnp.where(column % 2 == 0, jnp.cos(angles), jnp.sin(angles)) * jnp.float32(
        1.0 / math.sqrt(length)
    )
    return values.astype(jnp.bfloat16)


def block_turns(total):
    turns = max(1, total // 2048)
    while total % turns != 0:
        turns = turns - 1
    return turns


def shards(signal, weight, cycle, phi, psi, owner, wigner):
    groups = lax.axis_size("blk")
    beams = lax.axis_size("beam")
    blocks = owner.shape[0]
    capacity = max(2, 5 * blocks // (2 * groups))
    slots = capacity * BLOCK_ROWS
    target_group = owner[:, 0]
    hits = (target_group[:, None] == jnp.arange(groups, dtype=jnp.int32)[None, :]).astype(jnp.int32)
    earlier = jnp.cumsum(hits, axis=0) - hits
    within = jnp.sum(earlier * hits, axis=1)
    position = target_group * capacity + within
    source = (
        jnp.zeros((groups * capacity,), jnp.int32)
        .at[position]
        .set(jnp.arange(blocks, dtype=jnp.int32))
    )
    filled = jnp.zeros((groups * capacity,), jnp.int32).at[position].set(1)

    def arrange(data):
        leading = data.shape[0]
        shaped = data.reshape(leading, blocks, BLOCK_ROWS)
        taken = jnp.take(shaped, source, axis=1)
        taken = jnp.where(filled[None, :, None] > 0, taken, jnp.zeros_like(taken))
        return taken.reshape(leading, groups, slots)

    sample_value = signal * weight
    packed = (cycle * NPSI + psi) * NPHI + phi
    total = groups * slots
    beam_rows = (psi_rows(psi, NPSI) * sample_value[None, :]).astype(jnp.bfloat16)
    got_rows, got_code = (
        lax.all_to_all(arrange(beam_rows), "blk", split_axis=1, concat_axis=1, tiled=True),
        lax.all_to_all(arrange(packed[None, :]), "blk", split_axis=1, concat_axis=1, tiled=True),
    )
    received = got_rows.reshape(NPSI, total)
    codes = got_code.reshape(total)
    cycle_of = codes // (NPSI * NPHI)
    phi_of = codes % NPHI
    spread = jnp.concatenate(
        [
            jnp.where(cycle_of[None, :] == level, received, jnp.zeros_like(received))
            for level in range(CYCLE_DEV)
        ],
        axis=0,
    )
    turns = block_turns(total)
    width = total // turns
    columns = jnp.arange(NPHI, dtype=jnp.int32)

    def bin_block(number, carry):
        start = number * width
        part = lax.dynamic_slice_in_dim(spread, start, width, 1)
        place = lax.dynamic_slice_in_dim(phi_of, start, width, 0)
        onehot = (place[:, None] == columns[None, :]).astype(jnp.bfloat16)
        return carry + jnp.dot(part, onehot, preferred_element_type=jnp.float32)

    cube = lax.fori_loop(0, turns, bin_block, jnp.zeros((CYCLE_DEV * NPSI, NPHI), jnp.float32))
    cube = cube.reshape(CYCLE_DEV, NPSI, NPHI)
    share = NPSI // beams
    summed = lax.psum(cube.astype(jnp.bfloat16), "beam").astype(jnp.float32)
    mine = lax.dynamic_slice_in_dim(summed, lax.axis_index("beam") * share, share, 1)
    spectra = jnp.dot(
        mine.astype(jnp.bfloat16).reshape(CYCLE_DEV * share, NPHI),
        phi_table(NPHI),
        preferred_element_type=jnp.float32,
    )
    spectra = spectra.astype(jnp.bfloat16).reshape(CYCLE_DEV, share, NPHI)
    regrouped = lax.all_to_all(spectra, "blk", split_axis=2, concat_axis=0, tiled=True)
    orders = regrouped.shape[2] // 2
    coeffs = regrouped.reshape(regrouped.shape[0], share, orders, 2).transpose(2, 1, 0, 3)
    partial_sum = jnp.einsum("mqtl,mqtp->mpl", wigner, coeffs, preferred_element_type=jnp.float32)
    totals = lax.psum(partial_sum.astype(jnp.bfloat16), "beam").astype(jnp.float32)
    return lax.dynamic_slice_in_dim(
        totals, lax.axis_index("beam") * (orders // beams), orders // beams, 0
    )


def solution(mesh):
    return jax.shard_map(
        shards,
        mesh=mesh,
        in_specs=(
            P(("blk", "beam")),
            P(("blk", "beam")),
            P(("blk", "beam")),
            P(("blk", "beam")),
            P(("blk", "beam")),
            P(("blk", "beam"), None),
            P("blk", "beam", None, None),
        ),
        out_specs=P(("blk", "beam"), None, None),
        check_vma=False,
    )
```

profile of v0, /device:TPU:1, one launch (start us, length us, event | category | flops | bytes accessed | tf_op | source)
XLA Modules:
  0.0 403.6 jit_solution(6288089818550073363)
XLA Ops:
  14.4 8.6 %all-to-all-start = ((s32[1,16,2560]{2,0,1:T(1,128)}), s32[1,16,2560]{2,0,1:T(1,128)S(1)}, u32[]{:S(2)}, u32[]{:S(2)}) async-start(s32[1,16,2560]{2,0,1:T(1,128)} %copy.19), calls=%async_computation | async-start | bytes 327680 | tf_op jit(solution)/shard_map/all_to_all | solution.py:74
  23.3 9.4 %multiply_convert_fusion.4 = bf16[32,128,128]{2,0,1:T(8,128)(2,1)} fusion(f32[128,128]{1,0:T(8,128)S(1)} %multiply_bitcast_fusion, s32[128,128]{1,0:T(8,128)S(1)} %bitcast.56, s32[32]{0:T(128)S(1)} %add_select_fusion.6, pred[32]{0:T(512)(128)(4,1)S(1)} %iota_compare_fusion.5), kind=kLoop, calls=%fused_computation.38 | loop fusion | flops 8912896 | bytes 1179808 | tf_op jit(solution)/shard_map/convert_element_type | solution.py:71
  37.6 4.9 %gather.15 = bf16[32,16,2560]{2,1,0:T(8,128)(2,1)S(1)} reshape(bf16[32,320,128]{2,1,0:T(8,128)(2,1)} %copy.20) | data formatting | bytes 5242880 | tf_op jit(solution)/shard_map/jit(_take)/gather | solution.py:64
  46.2 6.7 %all-to-all-start.1 = ((bf16[32,16,2560]{2,0,1:T(8,128)(2,1)}), bf16[32,16,2560]{2,0,1:T(8,128)(2,1)S(1)}, u32[]{:S(2)}, u32[]{:S(2)}) async-start(bf16[32,16,2560]{2,0,1:T(8,128)(2,1)} %copy.21), calls=%async_computation.1 | async-start | bytes 5242880 | tf_op jit(solution)/shard_map/all_to_all | solution.py:73
  53.3 31.6 %all-to-all-done.1 = bf16[32,16,2560]{2,0,1:T(8,128)(2,1)S(1)} async-done(((bf16[32,16,2560]{2,0,1:T(8,128)(2,1)}), bf16[32,16,2560]{2,0,1:T(8,128)(2,1)S(1)}, u32[]{:S(2)}, u32[]{:S(2)}) %all-to-all-start.1) | async-done | bytes 2621472 | tf_op jit(solution)/shard_map/all_to_all | solution.py:73
  88.6 90.4 %while.14 = (s32[]{:T(128)}, f32[64,2048]{1,0:T(8,128)S(1)}, bf16[64,40960]{1,0:T(8,128)(2,1)}, s32[40960]{0:T(1024)S(1)}, s32[]{:T(128)}, /*index=5*/s32[]{:T(128)}, s32[]{:T(128)}, s32[]{:T(128)}) while((s32[]{:T(128)}, f32[64,2048]{1,0:T(8,128)S(1)}, bf16[64,40960]{1,0:T(8,128)(2,1)}, s32[40960]{0:T(1024)S(1)}, s32[]{:T(128)}, ...), condition=%wide.region_5.6_spmd.clone, body=%wide.region_4.5_spmd.clone.sunk | while | flops 541327360 | bytes 1335445 | solution.py:98
  93.1 4.5 %fusion.46 = f32[64,2048]{1,0:T(8,128)S(1)} fusion(s32[2048]{0:T(1024)S(1)} %dynamic_slice.33, f32[64,2048]{1,0:T(8,128)S(1)} %get-tuple-element.165, bf16[64,40960]{1,0:T(8,128)(2,1)} %get-tuple-element.174, s32[]{:T(128)S(6)} %select_n.210, pred[]{:T(512)S(6)} %compare.24), kind=kOutput, calls=%fused_computation.8.clone.1 | convolution fusion | flops 541327360 | bytes 1318917 | tf_op jit(solution)/shard_map/while/body/eval_jaxpr/dot_general | solution.py:96
  97.7 4.5 %fusion.46 = f32[64,2048]{1,0:T(8,128)S(1)} fusion(s32[2048]{0:T(1024)S(1)} %dynamic_slice.33, f32[64,2048]{1,0:T(8,128)S(1)} %get-tuple-element.165, bf16[64,40960]{1,0:T(8,128)(2,1)} %get-tuple-element.174, s32[]{:T(128)S(6)} %select_n.210, pred[]{:T(512)S(6)} %compare.24), kind=kOutput, calls=%fused_computation.8.clone.1 | convolution fusion | flops 541327360 | bytes 1318917 | tf_op jit(solution)/shard_map/while/body/eval_jaxpr/dot_general | solution.py:96
  102.2 4.5 %fusion.46 = f32[64,2048]{1,0:T(8,128)S(1)} fusion(s32[2048]{0:T(1024)S(1)} %dynamic_slice.33, f32[64,2048]{1,0:T(8,128)S(1)} %get-tuple-element.165, bf16[64,40960]{1,0:T(8,128)(2,1)} %get-tuple-element.174, s32[]{:T(128)S(6)} %select_n.210, pred[]{:T(512)S(6)} %compare.24), kind=kOutput, calls=%fused_computation.8.clone.1 | convolution fusion | flops 541327360 | bytes 1318917 | tf_op jit(solution)/shard_map/while/body/eval_jaxpr/dot_general | solution.py:96
  106.7 4.5 %fusion.46 = f32[64,2048]{1,0:T(8,128)S(1)} fusion(s32[2048]{0:T(1024)S(1)} %dynamic_slice.33, f32[64,2048]{1,0:T(8,128)S(1)} %get-tuple-element.165, bf16[64,40960]{1,0:T(8,128)(2,1)} %get-tuple-element.174, s32[]{:T(128)S(6)} %select_n.210, pred[]{:T(512)S(6)} %compare.24), kind=kOutput, calls=%fused_computation.8.clone.1 | convolution fusion | flops 541327360 | bytes 1318917 | tf_op jit(solution)/shard_map/while/body/eval_jaxpr/dot_general | solution.py:96
  111.2 4.5 %fusion.46 = f32[64,2048]{1,0:T(8,128)S(1)} fusion(s32[2048]{0:T(1024)S(1)} %dynamic_slice.33, f32[64,2048]{1,0:T(8,128)S(1)} %get-tuple-element.165, bf16[64,40960]{1,0:T(8,128)(2,1)} %get-tuple-element.174, s32[]{:T(128)S(6)} %select_n.210, pred[]{:T(512)S(6)} %compare.24), kind=kOutput, calls=%fused_computation.8.clone.1 | convolution fusion | flops 541327360 | bytes 1318917 | tf_op jit(solution)/shard_map/while/body/eval_jaxpr/dot_general | solution.py:96
  124.8 4.5 %fusion.46 = f32[64,2048]{1,0:T(8,128)S(1)} fusion(s32[2048]{0:T(1024)S(1)} %dynamic_slice.33, f32[64,2048]{1,0:T(8,128)S(1)} %get-tuple-element.165, bf16[64,40960]{1,0:T(8,128)(2,1)} %get-tuple-element.174, s32[]{:T(128)S(6)} %select_n.210, pred[]{:T(512)S(6)} %compare.24), kind=kOutput, calls=%fused_computation.8.clone.1 | convolution fusion | flops 541327360 | bytes 1318917 | tf_op jit(solution)/shard_map/while/body/eval_jaxpr/dot_general | solution.py:96
  129.3 4.5 %fusion.46 = f32[64,2048]{1,0:T(8,128)S(1)} fusion(s32[2048]{0:T(1024)S(1)} %dynamic_slice.33, f32[64,2048]{1,0:T(8,128)S(1)} %get-tuple-element.165, bf16[64,40960]{1,0:T(8,128)(2,1)} %get-tuple-element.174, s32[]{:T(128)S(6)} %select_n.210, pred[]{:T(512)S(6)} %compare.24), kind=kOutput, calls=%fused_computation.8.clone.1 | convolution fusion | flops 541327360 | bytes 1318917 | tf_op jit(solution)/shard_map/while/body/eval_jaxpr/dot_general | solution.py:96
  138.3 4.5 %fusion.46 = f32[64,2048]{1,0:T(8,128)S(1)} fusion(s32[2048]{0:T(1024)S(1)} %dynamic_slice.33, f32[64,2048]{1,0:T(8,128)S(1)} %get-tuple-element.165, bf16[64,40960]{1,0:T(8,128)(2,1)} %get-tuple-element.174, s32[]{:T(128)S(6)} %select_n.210, pred[]{:T(512)S(6)} %compare.24), kind=kOutput, calls=%fused_computation.8.clone.1 | convolution fusion | flops 541327360 | bytes 1318917 | tf_op jit(solution)/shard_map/while/body/eval_jaxpr/dot_general | solution.py:96
  142.9 4.5 %fusion.46 = f32[64,2048]{1,0:T(8,128)S(1)} fusion(s32[2048]{0:T(1024)S(1)} %dynamic_slice.33, f32[64,2048]{1,0:T(8,128)S(1)} %get-tuple-element.165, bf16[64,40960]{1,0:T(8,128)(2,1)} %get-tuple-element.174, s32[]{:T(128)S(6)} %select_n.210, pred[]{:T(512)S(6)} %compare.24), kind=kOutput, calls=%fused_computation.8.clone.1 | convolution fusion | flops 541327360 | bytes 1318917 | tf_op jit(solution)/shard_map/while/body/eval_jaxpr/dot_general | solution.py:96
  147.4 4.5 %fusion.46 = f32[64,2048]{1,0:T(8,128)S(1)} fusion(s32[2048]{0:T(1024)S(1)} %dynamic_slice.33, f32[64,2048]{1,0:T(8,128)S(1)} %get-tuple-element.165, bf16[64,40960]{1,0:T(8,128)(2,1)} %get-tuple-element.174, s32[]{:T(128)S(6)} %select_n.210, pred[]{:T(512)S(6)} %compare.24), kind=kOutput, calls=%fused_computation.8.clone.1 | convolution fusion | flops 541327360 | bytes 1318917 | tf_op jit(solution)/shard_map/while/body/eval_jaxpr/dot_general | solution.py:96
  156.4 4.5 %fusion.46 = f32[64,2048]{1,0:T(8,128)S(1)} fusion(s32[2048]{0:T(1024)S(1)} %dynamic_slice.33, f32[64,2048]{1,0:T(8,128)S(1)} %get-tuple-element.165, bf16[64,40960]{1,0:T(8,128)(2,1)} %get-tuple-element.174, s32[]{:T(128)S(6)} %select_n.210, pred[]{:T(512)S(6)} %compare.24), kind=kOutput, calls=%fused_computation.8.clone.1 | convolution fusion | flops 541327360 | bytes 1318917 | tf_op jit(solution)/shard_map/while/body/eval_jaxpr/dot_general | solution.py:96
  161.0 4.5 %fusion.46 = f32[64,2048]{1,0:T(8,128)S(1)} fusion(s32[2048]{0:T(1024)S(1)} %dynamic_slice.33, f32[64,2048]{1,0:T(8,128)S(1)} %get-tuple-element.165, bf16[64,40960]{1,0:T(8,128)(2,1)} %get-tuple-element.174, s32[]{:T(128)S(6)} %select_n.210, pred[]{:T(512)S(6)} %compare.24), kind=kOutput, calls=%fused_computation.8.clone.1 | convolution fusion | flops 541327360 | bytes 1318917 | tf_op jit(solution)/shard_map/while/body/eval_jaxpr/dot_general | solution.py:96
  174.5 4.5 %fusion.46 = f32[64,2048]{1,0:T(8,128)S(1)} fusion(s32[2048]{0:T(1024)S(1)} %dynamic_slice.33, f32[64,2048]{1,0:T(8,128)S(1)} %get-tuple-element.165, bf16[64,40960]{1,0:T(8,128)(2,1)} %get-tuple-element.174, s32[]{:T(128)S(6)} %select_n.210, pred[]{:T(512)S(6)} %compare.24), kind=kOutput, calls=%fused_computation.8.clone.1 | convolution fusion | flops 541327360 | bytes 1318917 | tf_op jit(solution)/shard_map/while/body/eval_jaxpr/dot_general | solution.py:96
  179.8 60.6 %all-reduce.3.cloned.1.call-done = bf16[2,32,2048]{2,1,0:T(8,128)(2,1)} async-done(((bf16[2,32,2048]{2,1,0:T(8,128)(2,1)}), bf16[2,32,2048]{2,1,0:T(8,128)(2,1)}) %all-reduce.3.cloned.1.call-update) | async-done | bytes 262160 | tf_op jit(solution)/shard_map/psum | solution.py:101
  241.4 67.4 %fusion.16 = bf16[8,2048]{1,0:T(8,128)(2,1)S(1)} fusion(bf16[8,2048]{1,0:T(8,128)(2,1)S(1)} %reshape.216, s32[2048]{0:T(1024)S(1)} %add_select_fusion.4, pred[2048]{0:T(1024)(128)(4,1)S(1)} %fusion.24), kind=kOutput, calls=%fused_computation.34 | convolution fusion | flops 138428416 | bytes 75776 | tf_op jit(solution)/shard_map/dot_general | solution.py:103
  311.8 13.0 %all_to_all.25 = bf16[16,2,512]{2,1,0:T(2,128)(2,1)S(1)} all-to-all(bf16[16,2,512]{2,1,0:T(2,128)(2,1)S(1)} %reshape.262), channel_id=1, replica_groups=mesh['blk'=16,'beam'=8] {'blk'}, dimensions={0} | all-to-all | bytes 65536 | tf_op jit(solution)/shard_map/all_to_all | solution.py:109
  328.8 10.0 %fusion.15 = bf16[64,2,1152]{2,1,0:T(2,128)(2,1)} fusion(bf16[64,4,32,1152]{3,2,1,0:T(8,128)(2,1)} %param.15, bf16[32,4,64,2]{0,3,1,2:T(2,128)(2,1)S(1)} %copy.26), kind=kOutput, calls=%fused_computation.33 | convolution fusion | flops 37896192 | bytes 19202048 | tf_op jit(solution)/shard_map/mqtl,mqtp->mpl/dot_general | solution.py:112
  338.8 56.5 %all-reduce.5.cloned.1.call-done = bf16[64,2,1152]{2,1,0:T(2,128)(2,1)} async-done(((bf16[64,2,1152]{2,1,0:T(2,128)(2,1)}), bf16[64,2,1152]{2,1,0:T(2,128)(2,1)}) %all-reduce.5.cloned.1.call-update) | async-done | bytes 294928 | tf_op jit(solution)/shard_map/psum | solution.py:113
  (89 shorter events, 62.2 us)
Async XLA Ops:
  6.5 16.8 %copy-start.2 = (s32[16384]{0:T(1024)S(1)}, s32[16384]{0:T(1024)}, u32[]{:S(2)}) copy-start(s32[16384]{0:T(1024)} %param.13) | copy-start | bytes 196612
  6.5 16.7 %copy-start.1 = (f32[16384]{0:T(1024)S(1)}, f32[16384]{0:T(1024)}, u32[]{:S(2)}) copy-start(f32[16384]{0:T(1024)} %param.10) | copy-start | bytes 196612
  6.5 16.7 %copy-start = (f32[16384]{0:T(1024)S(1)}, f32[16384]{0:T(1024)}, u32[]{:S(2)}) copy-start(f32[16384]{0:T(1024)} %param.9) | copy-start | bytes 196612
  14.4 31.7 %all-to-all-start = ((s32[1,16,2560]{2,0,1:T(1,128)}), s32[1,16,2560]{2,0,1:T(1,128)S(1)}, u32[]{:S(2)}, u32[]{:S(2)}) async-start(s32[1,16,2560]{2,0,1:T(1,128)} %copy.19), calls=%async_computation | async-start | bytes 327680 | tf_op jit(solution)/shard_map/all_to_all | solution.py:74
  46.2 38.7 %all-to-all-start.1 = ((bf16[32,16,2560]{2,0,1:T(8,128)(2,1)}), bf16[32,16,2560]{2,0,1:T(8,128)(2,1)S(1)}, u32[]{:S(2)}, u32[]{:S(2)}) async-start(bf16[32,16,2560]{2,0,1:T(8,128)(2,1)} %copy.21), calls=%async_computation.1 | async-start | bytes 5242880 | tf_op jit(solution)/shard_map/all_to_all | solution.py:73
  52.8 187.6 %all-reduce.3.cloned.1.call-start = ((), (), s32[]{:S(2)}) async-start(), calls=%async_computation.3 | async-start | bytes 524288 | tf_op jit(solution)/shard_map/psum | solution.py:101
  179.8 215.6 %all-reduce.5.cloned.1.call-start = ((), (), s32[]{:S(2)}) async-start(), calls=%async_computation.4 | async-start | bytes 589824 | tf_op jit(solution)/shard_map/psum | solution.py:113
Sparse Core Ops, SparseCore 0:
  179.9 60.5 all-reduce.2
  339.0 56.3 all-reduce.4
where the time goes:
time: 407 us; the launch traced here: 404 us
  matrix products  167 us (41%)
  waiting for transfers between devices  149 us (37%)
  local copies, waits for them, and re-layouts  25 us (6%)
  other arithmetic  20 us (5%)
  starting transfers between devices  15.5 us (4%)
  between operations  13.8 us (3%)
  blocking collectives  13 us (3%)
    dot_general x20, matrix products, bin_block(): return carry + jnp.dot(part, onehot, preferred_element_type=jnp.float32)  89.4 us
    dot_general x1, matrix products, shards(): jnp.dot(mine.astype(jnp.bfloat16).reshape(CYCLE_DEV * share, NPHI), phi_t...  67.4 us
    psum x1, waiting for transfers between devices, shards(): summed = lax.psum(cube.astype(jnp.bfloat16), 'beam').astype(jnp.float32)  60.6 us
    psum x1, waiting for transfers between devices, shards(): lax.psum(partial_sum.astype(jnp.bfloat16), 'beam').astype(jnp.float32)  56.5 us
    all_to_all x1, waiting for transfers between devices, shards(): lax.all_to_all(arrange(beam_rows), 'blk', split_axis=1, concat_axis=1, ti...  31.6 us
    all_to_all x1, blocking collectives, shards(): lax.all_to_all(spectra, 'blk', split_axis=2, concat_axis=0, tiled=True)  13 us
    gather x5, local copies, waits for them, and re-layouts, arrange(): taken = jnp.take(shaped, source, axis=1)  10.9 us
    dot_general x1, matrix products, shards(): jnp.einsum('mqtl,mqtp->mpl', wigner, coeffs, preferred_element_type=jnp.f...  10 us
  transfers between devices with their start and end apart: 4, of which 3 were waited for; matrix products, arithmetic and copies ran while one was open for 6% of the time, Pallas kernels for 0%

commit v1 on v0

v1 whole, which is shorter than its diff:
```python
import functools
import math

import jax
import jax.numpy as jnp
import numpy as np
from jax import lax
from jax.experimental import pallas as pl
from jax.experimental.pallas import tpu as pltpu
from jax.sharding import PartitionSpec as P

MESH = pl.DeviceIdType.MESH
F32 = jnp.float32
BF16 = jnp.bfloat16
NG = 16
NB = 8
NPSI = 32
NPHI = 2048
CAP = 20
CHUNK = 4
NCH = CAP // CHUNK
ROWS = 16 * NCH
L = 1152


def tables():
    q = np.arange(NPSI)[:, None]
    j = np.arange(NPSI)[None, :]
    psi = np.where(
        q <= 16, np.cos(2 * math.pi * ((q * j) % 32) / 32), np.sin(2 * math.pi * (((q - 16) * j) % 32) / 32)
    ) / math.sqrt(32)
    psi2 = np.einsum("qj,tu,fg->qtfujg", psi, np.eye(2), np.eye(8)).reshape(512, 512)
    f1 = np.arange(64)[:, None]
    r = np.arange(64)[None, :]
    angle = 2 * math.pi * ((r * f1) % 64) / 64
    cs = np.stack([np.cos(angle), np.sin(angle)], axis=1)
    cs = np.repeat(cs[:, :, :, None], 2, axis=3).reshape(64, 256)
    t1 = np.einsum("ab,fn->afbn", np.eye(4), cs).reshape(256, 1024)
    f0 = np.arange(32)[:, None]
    turn = 2 * math.pi * (r * f0) / 2048
    tr, ti = np.cos(turn) / math.sqrt(NPHI), np.sin(turn) / math.sqrt(NPHI)
    a = np.stack([tr, ti], axis=2).reshape(4, 8, 128)
    b = np.stack([-ti, tr], axis=2).reshape(4, 8, 128)
    tw = np.stack([a, b], axis=1)
    blk = np.arange(NG)[:, None]
    outer = 2 * math.pi * ((blk * np.arange(32)[None, :]) % 32) / 32
    cos, sin = np.cos(outer).reshape(NG, 4, 8), np.sin(outer).reshape(NG, 4, 8)
    both = np.stack([cos, sin], axis=2)
    d2 = np.einsum("bayf,st->bsaytf", both, np.eye(8)).reshape(128, 512)
    row = np.arange(128)
    b_, q_, t_ = row // 8, row // 2 % 4, row % 2
    e = np.zeros((128, 128))
    e[row, q_ * 32 + 2 * b_ + t_] = 1
    return (
        jnp.asarray(psi2, BF16),
        jnp.asarray(t1, BF16),
        jnp.asarray(tw, F32),
        jnp.asarray(d2, BF16),
        jnp.asarray(e, BF16),
    )


def send_kernel(signal, weight, cycle, phi, psi, owner, out, data, sendbuf, send_sem, recv_sem):
    me, row = lax.axis_index("blk"), lax.axis_index("beam")
    barrier = pltpu.get_barrier_semaphore()

    def greet(i, c):
        pl.semaphore_signal(barrier, inc=1, device_id=(lax.rem(me + i, NG), row), device_id_type=MESH)
        return c

    lax.fori_loop(1, NG, greet, 0)
    value = signal[...] * weight[...]
    zero = jnp.zeros_like(value)
    cyc = cycle[...]
    cell = phi[...]
    data[0:128] = jnp.where(cyc == 0, value, zero).astype(BF16)
    data[128:256] = jnp.where(cyc == 0, zero, value).astype(BF16)
    data[256:384] = (psi[...] * 8 + (cell & 7) + 1).astype(F32).astype(BF16)
    data[384:512] = (((cell >> 3) & 3) * 64 + (cell >> 5) + 1).astype(F32).astype(BF16)
    own = owner[...]
    hit = lax.broadcasted_iota(jnp.int32, (NG, 128), 0) == own
    upper = lax.broadcasted_iota(jnp.int32, (128, 128), 0) < lax.broadcasted_iota(jnp.int32, (128, 128), 1)
    before = jnp.dot(
        jnp.where(hit, 1.0, 0.0).astype(BF16), jnp.where(upper, 1.0, 0.0).astype(BF16), preferred_element_type=F32
    )
    within = jnp.sum(jnp.where(hit, before, 0.0), axis=0, keepdims=True).astype(jnp.int32)
    key = own * 1024 + within
    key = jnp.concatenate([key, key + 32, key + 64, key + 96], axis=1)
    at = lax.broadcasted_iota(jnp.int32, (ROWS, 512), 0)
    base = ((at >> 4) * CHUNK + (at & 3)) + ((at >> 2) & 3) * 32
    pl.semaphore_wait(barrier, NG - 1)

    def copy(g):
        return pltpu.make_async_remote_copy(
            src_ref=sendbuf.at[g],
            dst_ref=out.at[me],
            send_sem=send_sem.at[g],
            recv_sem=recv_sem.at[me],
            device_id=(g, row),
            device_id_type=MESH,
        )

    def arrival(g):
        return pltpu.make_async_remote_copy(
            src_ref=sendbuf.at[g],
            dst_ref=out.at[g],
            send_sem=send_sem.at[g],
            recv_sem=recv_sem.at[g],
            device_id=(g, row),
            device_id_type=MESH,
        )

    def rows_of(g):
        chosen = jnp.where(base == key - g * 1024, 1.0, 0.0).astype(BF16)
        return jnp.dot(chosen, data[...], preferred_element_type=F32).astype(BF16)

    def send(i, c):
        g = lax.rem(me + i, NG)
        sendbuf[g] = rows_of(g)
        copy(g).start()
        return c

    lax.fori_loop(1, NG, send, 0)
    out[me] = rows_of(me)

    def settle(i, c):
        g = lax.rem(me + i, NG)
        copy(g).wait_send()
        arrival(g).wait_recv()
        return c

    lax.fori_loop(1, NG, settle, 0)


def bin_kernel(got, psi2, cube, acc, flag_v, flag_s, sem):
    flag_v[...] = got[...].astype(F32)[:, 8, :].astype(jnp.int32)
    move = pltpu.make_async_copy(flag_v, flag_s, sem)
    move.start()
    acc[...] = jnp.zeros_like(acc)
    move.wait()
    cells = (lax.broadcasted_iota(jnp.int32, (256, 128), 0) + 1).astype(F32).astype(BF16)
    one, zero = jnp.ones((256, 128), BF16), jnp.zeros((256, 128), BF16)

    def step(n, c):
        @pl.when(flag_s[n, 0] > 0)
        def _():
            tile = got[n]
            low, high, right = [], [], []
            for i in range(CHUNK):
                at = tile[8 + i : 9 + i] == cells
                low.append(jnp.where(at, jnp.broadcast_to(tile[i : i + 1], (256, 128)), zero))
                high.append(jnp.where(at, jnp.broadcast_to(tile[4 + i : 5 + i], (256, 128)), zero))
                right.append(jnp.where(tile[12 + i : 13 + i] == cells, one, zero))
            left = jnp.concatenate([jnp.concatenate(low, axis=1), jnp.concatenate(high, axis=1)], axis=0)
            acc[...] += lax.dot_general(
                left, jnp.concatenate(right, axis=1), (((1,), (1,)), ((), ())), preferred_element_type=F32
            )

        return c

    lax.fori_loop(0, NG * NCH, step, 0)
    cube[...] = jnp.dot(psi2[...], acc[...].astype(BF16), preferred_element_type=F32).astype(BF16)


def tail_kernel(
    cube, t1, tw, d2, perm, wigner, out,
    wig, got_a, mix, spec, got_c, coef, send_e, got_e,
    wig_sem, send_a, recv_a, send_c, recv_c, send_sem_e, recv_sem_e,
):
    blk, beam = lax.axis_index("blk"), lax.axis_index("beam")
    barrier = pltpu.get_barrier_semaphore()

    def load(e):
        rows = pl.ds(pl.multiple_of(e * 1024, 1024), 1024)
        return pltpu.make_async_copy(wigner.at[rows], wig.at[rows], wig_sem.at[e])

    def greet_blk(i, c):
        pl.semaphore_signal(barrier, inc=1, device_id=(lax.rem(blk + i, NG), beam), device_id_type=MESH)
        return c

    def greet_beam(i, c):
        pl.semaphore_signal(barrier, inc=1, device_id=(blk, lax.rem(beam + i, NB)), device_id_type=MESH)
        return c

    lax.fori_loop(1, NB, greet_beam, 0)
    lax.fori_loop(1, NG, greet_blk, 0)
    pl.semaphore_wait(barrier, NG + NB - 2)

    def copy_a(e, slot):
        return pltpu.make_async_remote_copy(
            src_ref=cube.at[pl.ds(pl.multiple_of(e * 64, 64), 64)],
            dst_ref=got_a.at[slot],
            send_sem=send_a.at[e],
            recv_sem=recv_a.at[slot],
            device_id=(blk, e),
            device_id_type=MESH,
        )

    def start_a(i, c):
        copy_a(lax.rem(beam + i, NB), beam).start()
        return c

    lax.fori_loop(1, NB, start_a, 0)

    def start_load(i, c):
        load(lax.rem(beam + i, NB)).start()
        return c

    lax.fori_loop(1, NB + 1, start_load, 0)
    mine = cube[pl.ds(pl.multiple_of(beam * 64, 64), 64), :].astype(F32)

    def settle_a(i, total):
        e = lax.rem(beam + i, NB)
        copy_a(e, e).wait_recv()
        return total + got_a[e].astype(F32)

    x = lax.fori_loop(1, NB, settle_a, mine).astype(BF16)
    pq = jnp.dot(x, t1[...], preferred_element_type=F32)
    for a in range(4):
        p = pq[:, a * 256 : a * 256 + 128].reshape(8, 8, 128)
        q = pq[:, a * 256 + 128 : a * 256 + 256].reshape(8, 8, 128)
        ta, tb = tw[a, 0][None], tw[a, 1][None]
        mix[a * 128 : a * 128 + 64] = (p * ta + q * tb).reshape(64, 128).astype(BF16)
        mix[a * 128 + 64 : a * 128 + 128] = (p * tb - q * ta).reshape(64, 128).astype(BF16)
    spec[...] = jnp.dot(d2[...], mix[...], preferred_element_type=F32).reshape(NG, 8, 128)

    def copy_c(g, slot):
        return pltpu.make_async_remote_copy(
            src_ref=spec.at[g],
            dst_ref=got_c.at[slot],
            send_sem=send_c.at[g],
            recv_sem=recv_c.at[slot],
            device_id=(g, beam),
            device_id_type=MESH,
        )

    def start_c(i, c):
        copy_c(lax.rem(blk + i, NG), blk).start()
        return c

    lax.fori_loop(1, NG, start_c, 0)
    got_c[blk] = spec[blk]

    def settle_c(i, c):
        g = lax.rem(blk + i, NG)
        copy_c(g, g).wait_recv()
        return c

    lax.fori_loop(1, NG, settle_c, 0)
    coef[...] = lax.dot_general(
        got_c[...].reshape(128, 128).astype(BF16), perm[...], (((0,), (0,)), ((), ())), preferred_element_type=F32
    ).astype(BF16)
    diagonal = (lax.broadcasted_iota(jnp.int32, (16, 1024), 0) >> 1) == (
        lax.broadcasted_iota(jnp.int32, (16, 1024), 1) >> 7
    )

    def copy_e(e, slot):
        return pltpu.make_async_remote_copy(
            src_ref=send_e.at[e],
            dst_ref=got_e.at[slot],
            send_sem=send_sem_e.at[e],
            recv_sem=recv_sem_e.at[slot],
            device_id=(blk, e),
            device_id_type=MESH,
        )

    def contract(i, c):
        e = lax.rem(beam + i, NB)
        load(e).wait()
        rows = coef[pl.ds(pl.multiple_of(e * 16, 16), 16), :].astype(F32)
        left = jnp.where(diagonal, jnp.concatenate([rows] * 8, axis=1), 0.0).astype(BF16)
        part = jnp.dot(left, wig[pl.ds(pl.multiple_of(e * 1024, 1024), 1024), :], preferred_element_type=F32)

        @pl.when(i < NB)
        def _():
            send_e[e] = part.astype(BF16)
            copy_e(e, beam).start()

        @pl.when(i == NB)
        def _():
            out[...] = part

        return c

    lax.fori_loop(1, NB + 1, contract, 0)

    def settle_e(i, c):
        e = lax.rem(beam + i, NB)
        copy_e(e, e).wait_recv()
        out[...] += got_e[e].astype(F32)
        return c

    lax.fori_loop(1, NB, settle_e, 0)

    def sent_beam(i, c):
        e = lax.rem(beam + i, NB)
        copy_a(e, e).wait_send()
        copy_e(e, e).wait_send()
        return c

    def sent_blk(i, c):
        g = lax.rem(blk + i, NG)
        copy_c(g, g).wait_send()
        return c

    lax.fori_loop(1, NB, sent_beam, 0)
    lax.fori_loop(1, NG, sent_blk, 0)


VMEM = functools.partial(pl.BlockSpec, memory_space=pltpu.VMEM)


def shards(signal, weight, cycle, phi, psi, owner, wigner):
    psi2, t1, tw, d2, perm = tables()
    block = lambda x: x.reshape(128, 128)
    dma = pltpu.SemaphoreType.DMA
    got = pl.pallas_call(
        send_kernel,
        out_shape=jax.ShapeDtypeStruct((NG, ROWS, 128), BF16),
        in_specs=[VMEM()] * 6,
        out_specs=VMEM(),
        scratch_shapes=[
            pltpu.VMEM((512, 128), BF16),
            pltpu.VMEM((NG, ROWS, 128), BF16),
            dma((NG,)),
            dma((NG,)),
        ],
        compiler_params=pltpu.CompilerParams(
            collective_id=0, has_side_effects=True, vmem_limit_bytes=16 * 2**20
        ),
        name="send_samples",
    )(block(signal), block(weight), block(cycle), block(phi), block(psi), owner.reshape(1, 128))
    cube = pl.pallas_call(
        bin_kernel,
        out_shape=jax.ShapeDtypeStruct((512, 256), BF16),
        in_specs=[VMEM()] * 2,
        out_specs=VMEM(),
        scratch_shapes=[
            pltpu.VMEM((512, 256), F32),
            pltpu.VMEM((NG * NCH, 128), jnp.int32),
            pltpu.SMEM((NG * NCH, 128), jnp.int32),
            dma,
        ],
        compiler_params=pltpu.CompilerParams(vmem_limit_bytes=24 * 2**20),
        name="bin_samples",
    )(got.reshape(NG * NCH, 16, 128), psi2)
    alm = pl.pallas_call(
        tail_kernel,
        out_shape=jax.ShapeDtypeStruct((16, L), F32),
        in_specs=[VMEM()] * 5 + [pl.BlockSpec(memory_space=pl.ANY)],
        out_specs=VMEM(),
        scratch_shapes=[
            pltpu.VMEM((64 * 128, L), BF16),
            pltpu.VMEM((NB, 64, 256), BF16),
            pltpu.VMEM((512, 128), BF16),
            pltpu.VMEM((NG, 8, 128), F32),
            pltpu.VMEM((NG, 8, 128), F32),
            pltpu.VMEM((128, 128), BF16),
            pltpu.VMEM((NB, 16, L), BF16),
            pltpu.VMEM((NB, 16, L), BF16),
            dma((NB,)),
            dma((NB,)),
            dma((NB,)),
            dma((NG,)),
            dma((NG,)),
            dma((NB,)),
            dma((NB,)),
        ],
        compiler_params=pltpu.CompilerParams(
            collective_id=1, has_side_effects=True, vmem_limit_bytes=40 * 2**20
        ),
        name="sky_coefficients",
    )(cube, t1, tw, d2, perm, wigner.reshape(64 * 128, L))
    return alm.reshape(8, 2, L)


def solution(mesh):
    return jax.shard_map(
        shards,
        mesh=mesh,
        in_specs=(
            P(("blk", "beam")),
            P(("blk", "beam")),
            P(("blk", "beam")),
            P(("blk", "beam")),
            P(("blk", "beam")),
            P(("blk", "beam"), None),
            P("blk", "beam", None, None),
        ),
        out_specs=P(("blk", "beam"), None, None),
        check_vma=False,
    )
```

time: 407 us -> 73.4 us (0.18)
  matrix products: 167 us -> 0 us
  waiting for transfers between devices: 149 us -> 0 us
  Pallas kernels: 0 us -> 62.8 us
  other arithmetic: 20 us -> 0 us
  starting transfers between devices: 15.5 us -> 0 us
  local copies, waits for them, and re-layouts: 25 us -> 10 us
  between operations: 13.8 us -> 0.05 us
  blocking collectives: 13 us -> 0 us
    dot_general x22 -> x0, matrix products: 167 us -> none  [the longest x20 89.4 us: bin_block(): return carry + jnp.dot(part, onehot, preferred_element_type=jnp.float32)]
    psum x2 -> x0, waiting for transfers between devices: 117 us -> none  [the longest x1 60.6 us: shards(): summed = lax.psum(cube.astype(jnp.bfloat16), 'beam').astype(jnp.float32)]
    pallas_call x0 -> x3, Pallas kernels: none -> 62.8 us  [the longest x1 26.3 us: shards(): pl.pallas_call(tail_kernel, out_shape=jax.ShapeDtypeStruct((16, L), F32),...]
    all_to_all x2 -> x0, waiting for transfers between devices: 31.6 us -> none  [the longest x1 31.6 us: shards(): lax.all_to_all(arrange(beam_rows), 'blk', split_axis=1, concat_axis=1, ti...]
    all_to_all x2 -> x0, starting transfers between devices: 15.3 us -> none  [the longest x1 8.6 us: shards(): lax.all_to_all(arrange(packed[None, :]), 'blk', split_axis=1, concat_axis...]
    convert_element_type x5 -> x0, other arithmetic: 13.2 us -> none  [the longest x1 9.38 us: shards(): (psi_rows(psi, NPSI) * sample_value[None, :]).astype(jnp.bfloat16)]
    all_to_all x1 -> x0, blocking collectives: 13 us -> none  [shards(): lax.all_to_all(spectra, 'blk', split_axis=2, concat_axis=0, tiled=True)]
    gather x5 -> x0, local copies, waits for them, and re-layouts: 10.9 us -> none  [arrange(): taken = jnp.take(shaped, source, axis=1)]
  transfers between devices with their start and end apart: 4 -> 0, of which waited for: 3 -> 0; matrix products, arithmetic and copies ran while one was open for 6% -> 0% of each run, Pallas kernels for 0% -> 0%
where the time goes in v1:
time: 73.4 us; the launch traced here: 72.8 us
  Pallas kernels  62.8 us (86%)
  local copies, waits for them, and re-layouts  10 us (14%)
    pallas_call x1, Pallas kernels, shards(): pl.pallas_call(tail_kernel, out_shape=jax.ShapeDtypeStruct((16, L), F32),...  26.3 us
    pallas_call x1, Pallas kernels, shards(): pl.pallas_call(bin_kernel, out_shape=jax.ShapeDtypeStruct((512, 256), BF1...  23.6 us
    pallas_call x1, Pallas kernels, shards(): pl.pallas_call(send_kernel, out_shape=jax.ShapeDtypeStruct((NG, ROWS, 128...  12.9 us
    unnamed x22, local copies, waits for them, and re-layouts  9.34 us

profile of v1, /device:TPU:1, one launch (start us, length us, event | category | flops | bytes accessed | tf_op | source)
XLA Modules:
  0.0 72.8 jit_solution(10252817988822164897)
XLA Ops:
  0.0 0.0 copy-start.3
  0.0 0.8 %copy-done.3 = f32[16384]{0:T(1024)S(1)} copy-done((f32[16384]{0:T(1024)S(1)}, f32[16384]{0:T(1024)}, u32[]{:S(2)}) %copy-start.3) | copy-done | bytes 65560
  0.8 0.0 copy-start.4
  0.8 0.8 %copy-done.4 = f32[16384]{0:T(1024)S(1)} copy-done((f32[16384]{0:T(1024)S(1)}, f32[16384]{0:T(1024)}, u32[]{:S(2)}) %copy-start.4) | copy-done | bytes 65560
  1.7 0.0 copy-start.5
  1.7 0.8 %copy-done.5 = s32[16384]{0:T(1024)S(1)} copy-done((s32[16384]{0:T(1024)S(1)}, s32[16384]{0:T(1024)}, u32[]{:S(2)}) %copy-start.5) | copy-done | bytes 65560
  2.5 0.0 copy-start.6
  2.5 0.8 %copy-done.6 = s32[16384]{0:T(1024)S(1)} copy-done((s32[16384]{0:T(1024)S(1)}, s32[16384]{0:T(1024)}, u32[]{:S(2)}) %copy-start.6) | copy-done | bytes 65560
  3.4 0.0 copy-start.7
  3.4 0.8 %copy-done.7 = s32[16384]{0:T(1024)S(1)} copy-done((s32[16384]{0:T(1024)S(1)}, s32[16384]{0:T(1024)}, u32[]{:S(2)}) %copy-start.7) | copy-done | bytes 65560
  4.2 0.0 copy-start.10
  4.2 0.7 copy-done.10
  4.9 12.9 %send_samples.1 = bf16[16,80,128]{2,1,0:T(8,128)(2,1)S(1)} custom-call(f32[128,128]{1,0:T(8,128)S(1)} %bitcast.9, f32[128,128]{1,0:T(8,128)S(1)} %bitcast.10, s32[128,128]{1,0:T(8,128)S(1)} %bitcast.11, s32[128,128]{1,0:T(8,128)S(1)} %bitcast.12, s32[128,128]{1,0:T(8,128)S(1)} %bitcast.13, s32[1,128]{1,0:T(1,128)S(1)} %bitcast.14), custom_call_target="tpu_custom_call" | custom-call | tf_op jit(solution)/shard_map/send_samples/pallas_call | solution.py:317
  17.7 0.0 copy-start.1
  17.7 1.0 %copy-done.1 = bf16[512,512]{1,0:T(8,128)(2,1)S(1)} copy-done((bf16[512,512]{1,0:T(8,128)(2,1)S(1)}, bf16[512,512]{1,0:T(8,128)(2,1)}, u32[]{:S(2)}) %copy-start.1) | copy-done | bytes 524312
  18.8 23.6 %bin_samples.1.cube = bf16[512,256]{1,0:T(8,128)(2,1)S(1)} custom-call(bf16[80,16,128]{2,1,0:T(8,128)(2,1)S(1)} %bitcast.8, bf16[512,512]{1,0:T(8,128)(2,1)S(1)} %copy-done.1), custom_call_target="tpu_custom_call" | custom-call | tf_op jit(solution)/shard_map/bin_samples/pallas_call | solution.py:333
  42.3 0.0 copy-start
  42.4 1.0 %copy-done = bf16[256,1024]{1,0:T(8,128)(2,1)S(1)} copy-done((bf16[256,1024]{1,0:T(8,128)(2,1)S(1)}, bf16[256,1024]{1,0:T(8,128)(2,1)}, u32[]{:S(2)}) %copy-start) | copy-done | bytes 524312
  43.4 0.0 copy-start.2
  43.4 0.9 %copy-done.2 = bf16[128,512]{1,0:T(8,128)(2,1)S(1)} copy-done((bf16[128,512]{1,0:T(8,128)(2,1)S(1)}, bf16[128,512]{1,0:T(8,128)(2,1)}, u32[]{:S(2)}) %copy-start.2) | copy-done | bytes 131096
  44.3 0.8 %copy-done.8 = bf16[128,128]{1,0:T(8,128)(2,1)S(1)} copy-done((bf16[128,128]{1,0:T(8,128)(2,1)S(1)}, bf16[128,128]{1,0:T(8,128)(2,1)}, u32[]{:S(2)}) %copy-start.8) | copy-done | bytes 32792
  45.1 0.8 %copy-done.9 = f32[4,2,8,128]{3,2,1,0:T(8,128)S(1)} copy-done((f32[4,2,8,128]{3,2,1,0:T(8,128)S(1)}, f32[4,2,8,128]{3,2,1,0:T(8,128)}, u32[]{:S(2)}) %copy-start.9) | copy-done | bytes 32792
  45.8 26.3 %sky_coefficients.1 = f32[16,1152]{1,0:T(8,128)S(1)} custom-call(bf16[512,256]{1,0:T(8,128)(2,1)S(1)} %bin_samples.1.cube, bf16[256,1024]{1,0:T(8,128)(2,1)S(1)} %copy-done, f32[4,2,8,128]{3,2,1,0:T(8,128)S(1)} %copy-done.9, bf16[128,512]{1,0:T(8,128)(2,1)S(1)} %copy-done.2, bf16[128,128]{1,0:T(8,128)(2,1)S(1)} %copy-done.8, bf16[8192,1152]{1,0:T(8,128)(2,1)} %bitcast.15), custom_call_target="tpu_custom_call" | custom-call | tf_op jit(solution)/shard_map/sky_coefficients/pallas_call | solution.py:347
  72.2 0.7 reshape.35
  (2 shorter events, 0.0 us)
Async XLA Ops:
  0.0 0.8 %copy-start.3 = (f32[16384]{0:T(1024)S(1)}, f32[16384]{0:T(1024)}, u32[]{:S(2)}) copy-start(f32[16384]{0:T(1024)} %param.12) | copy-start | bytes 196612
  0.8 0.8 %copy-start.4 = (f32[16384]{0:T(1024)S(1)}, f32[16384]{0:T(1024)}, u32[]{:S(2)}) copy-start(f32[16384]{0:T(1024)} %param.13) | copy-start | bytes 196612
  1.7 0.8 %copy-start.5 = (s32[16384]{0:T(1024)S(1)}, s32[16384]{0:T(1024)}, u32[]{:S(2)}) copy-start(s32[16384]{0:T(1024)} %param.14) | copy-start | bytes 196612
  2.5 0.8 %copy-start.6 = (s32[16384]{0:T(1024)S(1)}, s32[16384]{0:T(1024)}, u32[]{:S(2)}) copy-start(s32[16384]{0:T(1024)} %param.15) | copy-start | bytes 196612
  3.4 0.8 %copy-start.7 = (s32[16384]{0:T(1024)S(1)}, s32[16384]{0:T(1024)}, u32[]{:S(2)}) copy-start(s32[16384]{0:T(1024)} %param.16) | copy-start | bytes 196612
  4.2 0.7 copy-start.10
  17.7 1.0 %copy-start.1 = (bf16[512,512]{1,0:T(8,128)(2,1)S(1)}, bf16[512,512]{1,0:T(8,128)(2,1)}, u32[]{:S(2)}) copy-start(bf16[512,512]{1,0:T(8,128)(2,1)} %constant.10.clone.psi2) | copy-start | bytes 1572868
  42.3 1.0 %copy-start = (bf16[256,1024]{1,0:T(8,128)(2,1)S(1)}, bf16[256,1024]{1,0:T(8,128)(2,1)}, u32[]{:S(2)}) copy-start(bf16[256,1024]{1,0:T(8,128)(2,1)} %constant.11.clone.t1) | copy-start | bytes 1572868
  43.4 0.9 %copy-start.2 = (bf16[128,512]{1,0:T(8,128)(2,1)S(1)}, bf16[128,512]{1,0:T(8,128)(2,1)}, u32[]{:S(2)}) copy-start(bf16[128,512]{1,0:T(8,128)(2,1)} %constant.13.clone.d2) | copy-start | bytes 393220
  44.3 0.8 %copy-start.8 = (bf16[128,128]{1,0:T(8,128)(2,1)S(1)}, bf16[128,128]{1,0:T(8,128)(2,1)}, u32[]{:S(2)}) copy-start(bf16[128,128]{1,0:T(8,128)(2,1)} %constant.14.clone.perm) | copy-start | bytes 98308
  45.1 0.8 %copy-start.9 = (f32[4,2,8,128]{3,2,1,0:T(8,128)S(1)}, f32[4,2,8,128]{3,2,1,0:T(8,128)}, u32[]{:S(2)}) copy-start(f32[4,2,8,128]{3,2,1,0:T(8,128)} %constant.12.clone.tw) | copy-start | bytes 98308

commit v2 on v1

v2 whole, which is shorter than its diff:
```python
import math

import jax
import jax.numpy as jnp
import numpy as np
from jax import lax
from jax.experimental import pallas as pl
from jax.experimental.pallas import tpu as pltpu
from jax.sharding import PartitionSpec as P

MESH = pl.DeviceIdType.MESH
F32 = jnp.float32
BF16 = jnp.bfloat16
NG = 16
NB = 8
NPSI = 32
NPHI = 2048
CAP = 20
CHUNK = 4
NCH = CAP // CHUNK
ROWS = 16 * NCH
L = 1152


def tables():
    q = np.arange(NPSI)[:, None]
    j = np.arange(NPSI)[None, :]
    psi = np.where(
        q <= 16, np.cos(2 * math.pi * ((q * j) % 32) / 32), np.sin(2 * math.pi * (((q - 16) * j) % 32) / 32)
    ) / math.sqrt(32)
    psi2 = np.einsum("qj,tu,fg->qtfujg", psi, np.eye(2), np.eye(8)).reshape(512, 512)
    f1 = np.arange(64)[:, None]
    r = np.arange(64)[None, :]
    angle = 2 * math.pi * ((r * f1) % 64) / 64
    cs = np.stack([np.cos(angle), np.sin(angle)], axis=1)
    cs = np.repeat(cs[:, :, :, None], 2, axis=3).reshape(64, 256)
    t1 = np.einsum("ab,fn->afbn", np.eye(4), cs).reshape(256, 1024)
    f0 = np.arange(32)[:, None]
    turn = 2 * math.pi * (r * f0) / 2048
    tr, ti = np.cos(turn) / math.sqrt(NPHI), np.sin(turn) / math.sqrt(NPHI)
    a = np.stack([tr, ti], axis=2).reshape(4, 8, 128)
    b = np.stack([-ti, tr], axis=2).reshape(4, 8, 128)
    tw = np.stack([a, b], axis=1)
    blk = np.arange(NG)[:, None]
    outer = 2 * math.pi * ((blk * np.arange(32)[None, :]) % 32) / 32
    cos, sin = np.cos(outer).reshape(NG, 4, 8), np.sin(outer).reshape(NG, 4, 8)
    both = np.stack([cos, sin], axis=2)
    d2 = np.einsum("bayf,st->bsaytf", both, np.eye(8)).reshape(128, 512)
    row = np.arange(128)
    b_, q_, t_ = row // 8, row // 2 % 4, row % 2
    e = np.zeros((128, 128))
    e[row, q_ * 32 + 2 * b_ + t_] = 1
    return (
        jnp.asarray(psi2, BF16),
        jnp.asarray(t1, BF16),
        jnp.asarray(tw, F32),
        jnp.asarray(d2, BF16),
        jnp.asarray(e, BF16),
    )


def kernel(
    signal, weight, cycle, phi, psi, owner, psi2, t1, tw, d2, perm, wigner, out,
    signal_v, weight_v, cycle_v, phi_v, psi_v, owner_v, psi2_v, t1_v, tw_v, d2_v, perm_v, wig,
    data, sendbuf, got, acc, dense, cube, got_a, mix, spec, got_c, coef, send_e, got_e,
    in_sem, wig_sem, send_s, recv_s, send_a, recv_a, send_c, recv_c, send_sem_e, recv_sem_e,
):
    blk, beam = lax.axis_index("blk"), lax.axis_index("beam")
    barrier = pltpu.get_barrier_semaphore()

    sources = (signal, weight, cycle, phi, psi, owner, psi2, t1, tw, d2, perm)
    places = (signal_v, weight_v, cycle_v, phi_v, psi_v, owner_v, psi2_v, t1_v, tw_v, d2_v, perm_v)
    fetches = [pltpu.make_async_copy(a, b, in_sem.at[n]) for n, (a, b) in enumerate(zip(sources, places))]
    for fetch in fetches:
        fetch.start()

    def greet_blk(i, c):
        pl.semaphore_signal(barrier, inc=1, device_id=(lax.rem(blk + i, NG), beam), device_id_type=MESH)
        return c

    def greet_beam(i, c):
        pl.semaphore_signal(barrier, inc=1, device_id=(blk, lax.rem(beam + i, NB)), device_id_type=MESH)
        return c

    lax.fori_loop(1, NG, greet_blk, 0)
    lax.fori_loop(1, NB, greet_beam, 0)

    def load(e):
        rows = pl.ds(pl.multiple_of(e * 1024, 1024), 1024)
        return pltpu.make_async_copy(wigner.at[rows], wig.at[rows], wig_sem.at[e])

    def start_load(i, c):
        load(lax.rem(beam + i, NB)).start()
        return c

    lax.fori_loop(1, NB + 1, start_load, 0)

    for fetch in fetches[:6]:
        fetch.wait()
    value = signal_v[...] * weight_v[...]
    zero = jnp.zeros_like(value)
    cyc = cycle_v[...]
    cell = phi_v[...]
    data[0:128] = jnp.where(cyc == 0, value, zero).astype(BF16)
    data[128:256] = jnp.where(cyc == 0, zero, value).astype(BF16)
    data[256:384] = (psi_v[...] * 8 + (cell & 7) + 1).astype(F32).astype(BF16)
    data[384:512] = (((cell >> 3) & 3) * 64 + (cell >> 5) + 1).astype(F32).astype(BF16)
    own = owner_v[...]
    hit = lax.broadcasted_iota(jnp.int32, (NG, 128), 0) == own
    upper = lax.broadcasted_iota(jnp.int32, (128, 128), 0) < lax.broadcasted_iota(jnp.int32, (128, 128), 1)
    before = jnp.dot(
        jnp.where(hit, 1.0, 0.0).astype(BF16), jnp.where(upper, 1.0, 0.0).astype(BF16), preferred_element_type=F32
    )
    within = jnp.sum(jnp.where(hit, before, 0.0), axis=0, keepdims=True).astype(jnp.int32)
    key = own * 1024 + within
    key = jnp.concatenate([key, key + 32, key + 64, key + 96], axis=1)
    at = lax.broadcasted_iota(jnp.int32, (ROWS, 512), 0)
    base = ((at >> 4) * CHUNK + (at & 3)) + ((at >> 2) & 3) * 32

    def copy_s(g, slot):
        return pltpu.make_async_remote_copy(
            src_ref=sendbuf.at[g],
            dst_ref=got.at[slot],
            send_sem=send_s.at[g],
            recv_sem=recv_s.at[slot],
            device_id=(g, beam),
            device_id_type=MESH,
        )

    def rows_of(first, count):
        keys = [base + lax.rem(blk + first + n, NG) * 1024 for n in range(count)]
        chosen = jnp.where(jnp.concatenate(keys, axis=0) == key, 1.0, 0.0).astype(BF16)
        return jnp.dot(chosen, data[...], preferred_element_type=F32).astype(BF16)

    pl.semaphore_wait(barrier, NG + NB - 2)

    def send(i, c):
        rows = rows_of(i * 3 + 1, 3)
        for n in range(3):
            g = lax.rem(blk + i * 3 + 1 + n, NG)
            sendbuf[g] = rows[n * ROWS : (n + 1) * ROWS]
            copy_s(g, blk).start()
        return c

    lax.fori_loop(0, 5, send, 0)
    got[blk] = rows_of(0, 1)

    cells = (lax.broadcasted_iota(jnp.int32, (256, 128), 0) + 1).astype(F32).astype(BF16)
    one, nil = jnp.ones((256, 128), BF16), jnp.zeros((256, 128), BF16)

    def bin_two(first, second):
        low, high, right = [], [], []
        for source in (first, second):
            for n in range(NCH):
                tile = got[source, 16 * n : 16 * n + 16]
                for i in range(CHUNK):
                    same = tile[8 + i : 9 + i] == cells
                    low.append(jnp.where(same, jnp.broadcast_to(tile[i : i + 1], (256, 128)), nil))
                    high.append(jnp.where(same, jnp.broadcast_to(tile[4 + i : 5 + i], (256, 128)), nil))
                    right.append(jnp.where(tile[12 + i : 13 + i] == cells, one, nil))
        left = jnp.concatenate([jnp.concatenate(low, axis=1), jnp.concatenate(high, axis=1)], axis=0)
        return lax.dot_general(
            left, jnp.concatenate(right, axis=1), (((1,), (1,)), ((), ())), preferred_element_type=F32
        )

    acc[...] = jnp.zeros_like(acc)

    def bins(i, c):
        first = lax.rem(blk + NG - 2 * i, NG)
        second = lax.rem(blk + NG - 2 * i - 1, NG)

        @pl.when(i > 0)
        def _():
            copy_s(first, first).wait_recv()

        copy_s(second, second).wait_recv()
        acc[...] += bin_two(first, second)
        return c

    lax.fori_loop(0, NG // 2, bins, 0)
    dense[...] = acc[...].astype(BF16)
    for fetch in fetches[6:]:
        fetch.wait()

    def copy_a(e, slot):
        return pltpu.make_async_remote_copy(
            src_ref=cube.at[e],
            dst_ref=got_a.at[slot],
            send_sem=send_a.at[e],
            recv_sem=recv_a.at[slot],
            device_id=(blk, e),
            device_id_type=MESH,
        )

    def share(e):
        rows = psi2_v[pl.ds(pl.multiple_of(e * 64, 64), 64), :]
        return jnp.dot(rows, dense[...], preferred_element_type=F32)

    def start_a(i, c):
        e = lax.rem(beam + i, NB)
        cube[e] = share(e).astype(BF16)
        copy_a(e, beam).start()
        return c

    lax.fori_loop(1, NB, start_a, 0)

    def settle_a(i, total):
        e = lax.rem(beam + NB - i, NB)
        copy_a(e, e).wait_recv()
        return total + got_a[e].astype(F32)

    x = lax.fori_loop(1, NB, settle_a, share(beam)).astype(BF16)
    pq = jnp.dot(x, t1_v[...], preferred_element_type=F32)
    for a in range(4):
        p = pq[:, a * 256 : a * 256 + 128].reshape(8, 8, 128)
        q = pq[:, a * 256 + 128 : a * 256 + 256].reshape(8, 8, 128)
        ta, tb = tw_v[a, 0][None], tw_v[a, 1][None]
        mix[a * 128 : a * 128 + 64] = (p * ta + q * tb).reshape(64, 128).astype(BF16)
        mix[a * 128 + 64 : a * 128 + 128] = (p * tb - q * ta).reshape(64, 128).astype(BF16)
    spec[...] = jnp.dot(d2_v[...], mix[...], preferred_element_type=F32).reshape(NG, 8, 128)

    def copy_c(g, slot):
        return pltpu.make_async_remote_copy(
            src_ref=spec.at[g],
            dst_ref=got_c.at[slot],
            send_sem=send_c.at[g],
            recv_sem=recv_c.at[slot],
            device_id=(g, beam),
            device_id_type=MESH,
        )

    def start_c(i, c):
        copy_c(lax.rem(blk + i, NG), blk).start()
        return c

    lax.fori_loop(1, NG, start_c, 0)
    got_c[blk] = spec[blk]

    def settle_c(i, c):
        g = lax.rem(blk + NG - i, NG)
        copy_c(g, g).wait_recv()
        return c

    lax.fori_loop(1, NG, settle_c, 0)
    coef[...] = lax.dot_general(
        got_c[...].reshape(128, 128).astype(BF16), perm_v[...], (((0,), (0,)), ((), ())), preferred_element_type=F32
    ).astype(BF16)
    diagonal = (lax.broadcasted_iota(jnp.int32, (16, 1024), 0) >> 1) == (
        lax.broadcasted_iota(jnp.int32, (16, 1024), 1) >> 7
    )

    def copy_e(e, slot):
        return pltpu.make_async_remote_copy(
            src_ref=send_e.at[e],
            dst_ref=got_e.at[slot],
            send_sem=send_sem_e.at[e],
            recv_sem=recv_sem_e.at[slot],
            device_id=(blk, e),
            device_id_type=MESH,
        )

    def contract(i, c):
        e = lax.rem(beam + i, NB)
        load(e).wait()
        rows = coef[pl.ds(pl.multiple_of(e * 16, 16), 16), :].astype(F32)
        left = jnp.where(diagonal, jnp.concatenate([rows] * 8, axis=1), 0.0).astype(BF16)
        part = jnp.dot(left, wig[pl.ds(pl.multiple_of(e * 1024, 1024), 1024), :], preferred_element_type=F32)

        @pl.when(i < NB)
        def _():
            send_e[e] = part.astype(BF16)
            copy_e(e, beam).start()

        @pl.when(i == NB)
        def _():
            out[...] = part

        return c

    lax.fori_loop(1, NB + 1, contract, 0)

    def settle_e(i, c):
        e = lax.rem(beam + NB - i, NB)
        copy_e(e, e).wait_recv()
        out[...] += got_e[e].astype(F32)
        return c

    lax.fori_loop(1, NB, settle_e, 0)

    def sent_beam(i, c):
        e = lax.rem(beam + i, NB)
        copy_a(e, e).wait_send()
        copy_e(e, e).wait_send()
        return c

    def sent_blk(i, c):
        g = lax.rem(blk + i, NG)
        copy_s(g, g).wait_send()
        copy_c(g, g).wait_send()
        return c

    lax.fori_loop(1, NB, sent_beam, 0)
    lax.fori_loop(1, NG, sent_blk, 0)


ANY = pl.BlockSpec(memory_space=pl.ANY)


def shards(signal, weight, cycle, phi, psi, owner, wigner):
    block = lambda x: x.reshape(128, 128)
    dma = pltpu.SemaphoreType.DMA
    operands = (
        block(signal),
        block(weight),
        block(cycle),
        block(phi),
        block(psi),
        owner.reshape(1, 128),
        *tables(),
        wigner.reshape(64 * 128, L),
    )
    alm = pl.pallas_call(
        kernel,
        out_shape=jax.ShapeDtypeStruct((16, L), F32),
        in_specs=[ANY] * len(operands),
        out_specs=pl.BlockSpec(memory_space=pltpu.VMEM),
        scratch_shapes=[
            *(pltpu.VMEM(x.shape, x.dtype) for x in operands),
            pltpu.VMEM((512, 128), BF16),
            pltpu.VMEM((NG, ROWS, 128), BF16),
            pltpu.VMEM((NG, ROWS, 128), BF16),
            pltpu.VMEM((512, 256), F32),
            pltpu.VMEM((512, 256), BF16),
            pltpu.VMEM((NB, 64, 256), BF16),
            pltpu.VMEM((NB, 64, 256), BF16),
            pltpu.VMEM((512, 128), BF16),
            pltpu.VMEM((NG, 8, 128), F32),
            pltpu.VMEM((NG, 8, 128), F32),
            pltpu.VMEM((128, 128), BF16),
            pltpu.VMEM((NB, 16, L), BF16),
            pltpu.VMEM((NB, 16, L), BF16),
            dma((11,)),
            dma((NB,)),
            dma((NG,)),
            dma((NG,)),
            dma((NB,)),
            dma((NB,)),
            dma((NG,)),
            dma((NG,)),
            dma((NB,)),
            dma((NB,)),
        ],
        compiler_params=pltpu.CompilerParams(
            collective_id=0, has_side_effects=True, vmem_limit_bytes=56 * 2**20
        ),
        name="sky_coefficients",
    )(*operands)
    return alm.reshape(8, 2, L)


def solution(mesh):
    return jax.shard_map(
        shards,
        mesh=mesh,
        in_specs=(
            P(("blk", "beam")),
            P(("blk", "beam")),
            P(("blk", "beam")),
            P(("blk", "beam")),
            P(("blk", "beam")),
            P(("blk", "beam"), None),
            P("blk", "beam", None, None),
        ),
        out_specs=P(("blk", "beam"), None, None),
        check_vma=False,
    )
```

time: 73.4 us -> 44.3 us (0.60)
  Pallas kernels: 62.8 us -> 42.6 us
  local copies, waits for them, and re-layouts: 10 us -> 1.56 us
    pallas_call x3 -> x1, Pallas kernels: 62.8 us -> 42.6 us  [shards(): pl.pallas_call(kernel, out_shape=jax.ShapeDtypeStruct((16, L), F32), in_s...]
    unnamed x22 -> x0, local copies, waits for them, and re-layouts: 9.34 us -> none
    reshape x1, local copies, waits for them, and re-layouts: 0.68 us -> 1.56 us  [shards(): return alm.reshape(8, 2, L)]
where the time goes in v2:
time: 44.3 us; the launch traced here: 44.1 us
  Pallas kernels  42.6 us (96%)
  local copies, waits for them, and re-layouts  1.56 us (4%)
    pallas_call x1, Pallas kernels, shards(): pl.pallas_call(kernel, out_shape=jax.ShapeDtypeStruct((16, L), F32), in_s...  42.6 us
    reshape x1, local copies, waits for them, and re-layouts, shards(): return alm.reshape(8, 2, L)  1.56 us

profile of v2, /device:TPU:1, one launch (start us, length us, event | category | flops | bytes accessed | tf_op | source)
XLA Modules:
  0.0 44.1 jit_solution(18011367314047839040)
XLA Ops:
  0.0 42.6 %sky_coefficients.1 = f32[16,1152]{1,0:T(8,128)} custom-call(f32[128,128]{1,0:T(8,128)} %bitcast.8, f32[128,128]{1,0:T(8,128)} %bitcast.9, s32[128,128]{1,0:T(8,128)} %bitcast.10, s32[128,128]{1,0:T(8,128)} %bitcast.11, s32[128,128]{1,0:T(8,128)} %bitcast.12, s32[1,128]{1,0:T(1,128)} %bitcast.13, bf16[512,512]{1,0:T(8,128)(2,1)} %constant.10.clone.psi2, ...), custom_call_target="tpu_custom_call" | custom-call | tf_op jit(solution)/shard_map/sky_coefficients/pallas_call | solution.py:322
  42.6 1.6 %reshape.31 = f32[8,2,1152]{2,1,0:T(2,128)} reshape(f32[16,1152]{1,0:T(8,128)} %sky_coefficients.1) | data formatting | bytes 147456 | tf_op jit(solution)/shard_map/reshape | solution.py:358

commit v3 on v2

--- a/solution.py
+++ b/solution.py
@@ -71,7 +71,7 @@
     sources = (signal, weight, cycle, phi, psi, owner, psi2, t1, tw, d2, perm)
     places = (signal_v, weight_v, cycle_v, phi_v, psi_v, owner_v, psi2_v, t1_v, tw_v, d2_v, perm_v)
     fetches = [pltpu.make_async_copy(a, b, in_sem.at[n]) for n, (a, b) in enumerate(zip(sources, places))]
-    for fetch in fetches:
+    for fetch in fetches[5::-1]:
         fetch.start()
 
     def greet_blk(i, c):
@@ -92,8 +92,6 @@
     def start_load(i, c):
         load(lax.rem(beam + i, NB)).start()
         return c
-
-    lax.fori_loop(1, NB + 1, start_load, 0)
 
     for fetch in fetches[:6]:
         fetch.wait()
@@ -127,23 +125,24 @@
             device_id_type=MESH,
         )
 
-    def rows_of(first, count):
-        keys = [base + lax.rem(blk + first + n, NG) * 1024 for n in range(count)]
-        chosen = jnp.where(jnp.concatenate(keys, axis=0) == key, 1.0, 0.0).astype(BF16)
-        return jnp.dot(chosen, data[...], preferred_element_type=F32).astype(BF16)
-
+    def rows_of(i, c):
+        chosen = jnp.concatenate([base + (4 * i + n) * 1024 for n in range(4)], axis=0) == key
+        rows = jnp.dot(jnp.where(chosen, 1.0, 0.0).astype(BF16), data[...], preferred_element_type=F32)
+        sendbuf[pl.ds(4 * i, 4)] = rows.astype(BF16).reshape(4, ROWS, 128)
+        return c
+
+    lax.fori_loop(0, NG // 4, rows_of, 0)
     pl.semaphore_wait(barrier, NG + NB - 2)
 
     def send(i, c):
-        rows = rows_of(i * 3 + 1, 3)
-        for n in range(3):
-            g = lax.rem(blk + i * 3 + 1 + n, NG)
-            sendbuf[g] = rows[n * ROWS : (n + 1) * ROWS]
-            copy_s(g, blk).start()
-        return c
-
-    lax.fori_loop(0, 5, send, 0)
-    got[blk] = rows_of(0, 1)
+        copy_s(lax.rem(blk + i, NG), blk).start()
+        return c
+
+    lax.fori_loop(1, NG, send, 0)
+    got[blk] = sendbuf[blk]
+    for fetch in fetches[6:]:
+        fetch.start()
+    lax.fori_loop(1, NB + 1, start_load, 0)
 
     cells = (lax.broadcasted_iota(jnp.int32, (256, 128), 0) + 1).astype(F32).astype(BF16)
     one, nil = jnp.ones((256, 128), BF16), jnp.zeros((256, 128), BF16)
@@ -192,13 +191,12 @@
             device_id_type=MESH,
         )
 
-    def share(e):
-        rows = psi2_v[pl.ds(pl.multiple_of(e * 64, 64), 64), :]
-        return jnp.dot(rows, dense[...], preferred_element_type=F32)
+    cube[...] = (
+        jnp.dot(psi2_v[...], dense[...], preferred_element_type=F32).astype(BF16).reshape(NB, 64, 256)
+    )
 
     def start_a(i, c):
         e = lax.rem(beam + i, NB)
-        cube[e] = share(e).astype(BF16)
         copy_a(e, beam).start()
         return c
 
@@ -209,7 +207,7 @@
         copy_a(e, e).wait_recv()
         return total + got_a[e].astype(F32)
 
-    x = lax.fori_loop(1, NB, settle_a, share(beam)).astype(BF16)
+    x = lax.fori_loop(1, NB, settle_a, cube[beam].astype(F32)).astype(BF16)
     pq = jnp.dot(x, t1_v[...], preferred_element_type=F32)
     for a in range(4):
         p = pq[:, a * 256 : a * 256 + 128].reshape(8, 8, 128)
@@ -321,7 +319,7 @@
     )
     alm = pl.pallas_call(
         kernel,
-        out_shape=jax.ShapeDtypeStruct((16, L), F32),
+        out_shape=pltpu.VMEM((16, L), F32),
         in_specs=[ANY] * len(operands),
         out_specs=pl.BlockSpec(memory_space=pltpu.VMEM),
         scratch_shapes=[

time: 44.3 us -> 42.5 us (0.959)
  Pallas kernels: 42.6 us -> 41.7 us
  local copies, waits for them, and re-layouts: 1.56 us -> 0.68 us
    reshape x1, local copies, waits for them, and re-layouts: 1.56 us -> 0.68 us  [shards(): return alm.reshape(8, 2, L)]
    pallas_call x1, Pallas kernels: 42.6 us -> 41.7 us  [shards(): pl.pallas_call(kernel, out_shape=pltpu.VMEM((16, L), F32), in_specs=[ANY]...]
where the time goes in v3:
time: 42.5 us; the launch traced here: 42.4 us
  Pallas kernels  41.7 us (98%)
  local copies, waits for them, and re-layouts  0.68 us (2%)
    pallas_call x1, Pallas kernels, shards(): pl.pallas_call(kernel, out_shape=pltpu.VMEM((16, L), F32), in_specs=[ANY]...  41.7 us

profile of v3, /device:TPU:1, one launch (start us, length us, event | category | flops | bytes accessed | tf_op | source)
XLA Modules:
  0.0 42.4 jit_solution(10993193883036111445)
XLA Ops:
  0.0 41.7 %sky_coefficients.1 = f32[16,1152]{1,0:T(8,128)S(1)} custom-call(f32[128,128]{1,0:T(8,128)} %bitcast.8, f32[128,128]{1,0:T(8,128)} %bitcast.9, s32[128,128]{1,0:T(8,128)} %bitcast.10, s32[128,128]{1,0:T(8,128)} %bitcast.11, s32[128,128]{1,0:T(8,128)} %bitcast.12, s32[1,128]{1,0:T(1,128)} %bitcast.13, bf16[512,512]{1,0:T(8,128)(2,1)} %constant.10.clone.psi2, ...), custom_call_target="tpu_custom_call" | custom-call | tf_op jit(solution)/shard_map/sky_coefficients/pallas_call | solution.py:320
  41.7 0.7 %reshape.31 = f32[8,2,1152]{2,1,0:T(2,128)} reshape(f32[16,1152]{1,0:T(8,128)S(1)} %sky_coefficients.1) | data formatting | bytes 147456 | tf_op jit(solution)/shard_map/reshape | solution.py:356

commit v4 on v3

--- a/solution.py
+++ b/solution.py
@@ -93,7 +93,20 @@
         load(lax.rem(beam + i, NB)).start()
         return c
 
-    for fetch in fetches[:6]:
+    fetches[5].wait()
+    own = owner_v[...]
+    hit = lax.broadcasted_iota(jnp.int32, (NG, 128), 0) == own
+    upper = lax.broadcasted_iota(jnp.int32, (128, 128), 0) < lax.broadcasted_iota(jnp.int32, (128, 128), 1)
+    before = jnp.dot(
+        jnp.where(hit, 1.0, 0.0).astype(BF16), jnp.where(upper, 1.0, 0.0).astype(BF16), preferred_element_type=F32
+    )
+    within = jnp.sum(jnp.where(hit, before, 0.0), axis=0, keepdims=True).astype(jnp.int32)
+    key = own * 1024 + within
+    key = jnp.concatenate([key, key + 32, key + 64, key + 96], axis=1)
+    at = lax.broadcasted_iota(jnp.int32, (ROWS, 512), 0)
+    base = ((at >> 4) * CHUNK + (at & 3)) + ((at >> 2) & 3) * 32
+
+    for fetch in fetches[:5]:
         fetch.wait()
     value = signal_v[...] * weight_v[...]
     zero = jnp.zeros_like(value)
@@ -103,18 +116,6 @@
     data[128:256] = jnp.where(cyc == 0, zero, value).astype(BF16)
     data[256:384] = (psi_v[...] * 8 + (cell & 7) + 1).astype(F32).astype(BF16)
     data[384:512] = (((cell >> 3) & 3) * 64 + (cell >> 5) + 1).astype(F32).astype(BF16)
-    own = owner_v[...]
-    hit = lax.broadcasted_iota(jnp.int32, (NG, 128), 0) == own
-    upper = lax.broadcasted_iota(jnp.int32, (128, 128), 0) < lax.broadcasted_iota(jnp.int32, (128, 128), 1)
-    before = jnp.dot(
-        jnp.where(hit, 1.0, 0.0).astype(BF16), jnp.where(upper, 1.0, 0.0).astype(BF16), preferred_element_type=F32
-    )
-    within = jnp.sum(jnp.where(hit, before, 0.0), axis=0, keepdims=True).astype(jnp.int32)
-    key = own * 1024 + within
-    key = jnp.concatenate([key, key + 32, key + 64, key + 96], axis=1)
-    at = lax.broadcasted_iota(jnp.int32, (ROWS, 512), 0)
-    base = ((at >> 4) * CHUNK + (at & 3)) + ((at >> 2) & 3) * 32
-
     def copy_s(g, slot):
         return pltpu.make_async_remote_copy(
             src_ref=sendbuf.at[g],
@@ -147,9 +148,9 @@
     cells = (lax.broadcasted_iota(jnp.int32, (256, 128), 0) + 1).astype(F32).astype(BF16)
     one, nil = jnp.ones((256, 128), BF16), jnp.zeros((256, 128), BF16)
 
-    def bin_two(first, second):
+    def bins_of(sources):
         low, high, right = [], [], []
-        for source in (first, second):
+        for source in sources:
             for n in range(NCH):
                 tile = got[source, 16 * n : 16 * n + 16]
                 for i in range(CHUNK):
@@ -164,19 +165,24 @@
 
     acc[...] = jnp.zeros_like(acc)
 
-    def bins(i, c):
-        first = lax.rem(blk + NG - 2 * i, NG)
-        second = lax.rem(blk + NG - 2 * i - 1, NG)
-
-        @pl.when(i > 0)
-        def _():
-            copy_s(first, first).wait_recv()
-
-        copy_s(second, second).wait_recv()
-        acc[...] += bin_two(first, second)
-        return c
-
-    lax.fori_loop(0, NG // 2, bins, 0)
+    def bins(start, count):
+        def step(i, c):
+            sources = [lax.rem(blk + 2 * NG - start - count * i - n, NG) for n in range(count)]
+            for n, g in enumerate(sources):
+                if n == 0 and start == 0:
+
+                    @pl.when(i > 0)
+                    def _():
+                        copy_s(g, g).wait_recv()
+                else:
+                    copy_s(g, g).wait_recv()
+            acc[...] += bins_of(sources)
+            return c
+
+        return step
+
+    lax.fori_loop(0, 4, bins(0, 1), 0)
+    lax.fori_loop(0, 3, bins(4, 4), 0)
     dense[...] = acc[...].astype(BF16)
     for fetch in fetches[6:]:
         fetch.wait()
@@ -195,15 +201,20 @@
         jnp.dot(psi2_v[...], dense[...], preferred_element_type=F32).astype(BF16).reshape(NB, 64, 256)
     )
 
+    def far(i, sign):
+        step = jnp.where(i < 3, 2, jnp.where(i < 5, 1, jnp.where(i < 7, 3, 0)))
+        x, core = lax.div(beam, 2), lax.rem(beam, 2)
+        return lax.rem(x + 4 + sign * step, 4) * 2 + lax.rem(core + i, 2)
+
     def start_a(i, c):
-        e = lax.rem(beam + i, NB)
+        e = far(i, 1)
         copy_a(e, beam).start()
         return c
 
     lax.fori_loop(1, NB, start_a, 0)
 
     def settle_a(i, total):
-        e = lax.rem(beam + NB - i, NB)
+        e = far(i, -1)
         copy_a(e, e).wait_recv()
         return total + got_a[e].astype(F32)
 
@@ -258,7 +269,7 @@
         )
 
     def contract(i, c):
-        e = lax.rem(beam + i, NB)
+        e = far(i, 1)
         load(e).wait()
         rows = coef[pl.ds(pl.multiple_of(e * 16, 16), 16), :].astype(F32)
         left = jnp.where(diagonal, jnp.concatenate([rows] * 8, axis=1), 0.0).astype(BF16)
@@ -278,7 +289,7 @@
     lax.fori_loop(1, NB + 1, contract, 0)
 
     def settle_e(i, c):
-        e = lax.rem(beam + NB - i, NB)
+        e = far(i, -1)
         copy_e(e, e).wait_recv()
         out[...] += got_e[e].astype(F32)
         return c

time: 42.5 us -> 41.1 us (0.967)
  Pallas kernels: 41.7 us -> 40.3 us
    pallas_call x1, Pallas kernels: 41.7 us -> 40.3 us  [shards(): pl.pallas_call(kernel, out_shape=pltpu.VMEM((16, L), F32), in_specs=[ANY]...]
where the time goes in v4:
time: 41.1 us; the launch traced here: 40.9 us
  Pallas kernels  40.3 us (98%)
  local copies, waits for them, and re-layouts  0.68 us (2%)
    pallas_call x1, Pallas kernels, shards(): pl.pallas_call(kernel, out_shape=pltpu.VMEM((16, L), F32), in_specs=[ANY]...  40.3 us

profile of v4, /device:TPU:1, one launch (start us, length us, event | category | flops | bytes accessed | tf_op | source)
XLA Modules:
  0.0 40.9 jit_solution(17967846613283699240)
XLA Ops:
  0.0 40.3 %sky_coefficients.1 = f32[16,1152]{1,0:T(8,128)S(1)} custom-call(f32[128,128]{1,0:T(8,128)} %bitcast.8, f32[128,128]{1,0:T(8,128)} %bitcast.9, s32[128,128]{1,0:T(8,128)} %bitcast.10, s32[128,128]{1,0:T(8,128)} %bitcast.11, s32[128,128]{1,0:T(8,128)} %bitcast.12, s32[1,128]{1,0:T(1,128)} %bitcast.13, bf16[512,512]{1,0:T(8,128)(2,1)} %constant.10.clone.psi2, ...), custom_call_target="tpu_custom_call" | custom-call | tf_op jit(solution)/shard_map/sky_coefficients/pallas_call | solution.py:331
  40.3 0.7 %reshape.31 = f32[8,2,1152]{2,1,0:T(2,128)} reshape(f32[16,1152]{1,0:T(8,128)S(1)} %sky_coefficients.1) | data formatting | bytes 147456 | tf_op jit(solution)/shard_map/reshape | solution.py:367

commit v5 on v4

--- a/solution.py
+++ b/solution.py
@@ -28,7 +28,7 @@
     psi = np.where(
         q <= 16, np.cos(2 * math.pi * ((q * j) % 32) / 32), np.sin(2 * math.pi * (((q - 16) * j) % 32) / 32)
     ) / math.sqrt(32)
-    psi2 = np.einsum("qj,tu,fg->qtfujg", psi, np.eye(2), np.eye(8)).reshape(512, 512)
+    psi2 = np.einsum("qj,fg->qfjg", psi, np.eye(8)).reshape(256, 256)
     f1 = np.arange(64)[:, None]
     r = np.arange(64)[None, :]
     angle = 2 * math.pi * ((r * f1) % 64) / 64
@@ -47,7 +47,7 @@
     both = np.stack([cos, sin], axis=2)
     d2 = np.einsum("bayf,st->bsaytf", both, np.eye(8)).reshape(128, 512)
     row = np.arange(128)
-    b_, q_, t_ = row // 8, row // 2 % 4, row % 2
+    b_, t_, q_ = row // 8, row // 4 % 2, row % 4
     e = np.zeros((128, 128))
     e[row, q_ * 32 + 2 * b_ + t_] = 1
     return (
@@ -62,7 +62,7 @@
 def kernel(
     signal, weight, cycle, phi, psi, owner, psi2, t1, tw, d2, perm, wigner, out,
     signal_v, weight_v, cycle_v, phi_v, psi_v, owner_v, psi2_v, t1_v, tw_v, d2_v, perm_v, wig,
-    data, sendbuf, got, acc, dense, cube, got_a, mix, spec, got_c, coef, send_e, got_e,
+    data, sendbuf, got, acc, cube, got_a, mix, spec, got_c, coef, send_e, got_e,
     in_sem, wig_sem, send_s, recv_s, send_a, recv_a, send_c, recv_c, send_sem_e, recv_sem_e,
 ):
     blk, beam = lax.axis_index("blk"), lax.axis_index("beam")
@@ -182,10 +182,12 @@
         return step
 
     lax.fori_loop(0, 4, bins(0, 1), 0)
-    lax.fori_loop(0, 3, bins(4, 4), 0)
-    dense[...] = acc[...].astype(BF16)
+    lax.fori_loop(0, 2, bins(4, 6), 0)
     for fetch in fetches[6:]:
         fetch.wait()
+    for t in range(2):
+        half = jnp.dot(psi2_v[...], acc[256 * t : 256 * t + 256].astype(BF16), preferred_element_type=F32)
+        cube[:, 32 * t : 32 * t + 32, :] = half.astype(BF16).reshape(NB, 32, 256)
 
     def copy_a(e, slot):
         return pltpu.make_async_remote_copy(
@@ -196,10 +198,6 @@
             device_id=(blk, e),
             device_id_type=MESH,
         )
-
-    cube[...] = (
-        jnp.dot(psi2_v[...], dense[...], preferred_element_type=F32).astype(BF16).reshape(NB, 64, 256)
-    )
 
     def far(i, sign):
         step = jnp.where(i < 3, 2, jnp.where(i < 5, 1, jnp.where(i < 7, 3, 0)))
@@ -339,7 +337,6 @@
             pltpu.VMEM((NG, ROWS, 128), BF16),
             pltpu.VMEM((NG, ROWS, 128), BF16),
             pltpu.VMEM((512, 256), F32),
-            pltpu.VMEM((512, 256), BF16),
             pltpu.VMEM((NB, 64, 256), BF16),
             pltpu.VMEM((NB, 64, 256), BF16),
             pltpu.VMEM((512, 128), BF16),

time: 41.1 us -> 40.7 us (level)
  Pallas kernels: 40.3 us -> 39.8 us
    pallas_call x1, Pallas kernels: 40.3 us -> 39.8 us  [shards(): pl.pallas_call(kernel, out_shape=pltpu.VMEM((16, L), F32), in_specs=[ANY]...]
where the time goes in v5:
time: 40.7 us; the launch traced here: 40.5 us
  Pallas kernels  39.8 us (98%)
  local copies, waits for them, and re-layouts  0.68 us (2%)
    pallas_call x1, Pallas kernels, shards(): pl.pallas_call(kernel, out_shape=pltpu.VMEM((16, L), F32), in_specs=[ANY]...  39.8 us

profile of v5, /device:TPU:1, one launch (start us, length us, event | category | flops | bytes accessed | tf_op | source)
XLA Modules:
  0.0 40.5 jit_solution(5746050491932879894)
XLA Ops:
  0.0 39.8 %sky_coefficients.1 = f32[16,1152]{1,0:T(8,128)S(1)} custom-call(f32[128,128]{1,0:T(8,128)} %bitcast.8, f32[128,128]{1,0:T(8,128)} %bitcast.9, s32[128,128]{1,0:T(8,128)} %bitcast.10, s32[128,128]{1,0:T(8,128)} %bitcast.11, s32[128,128]{1,0:T(8,128)} %bitcast.12, s32[1,128]{1,0:T(1,128)} %bitcast.13, bf16[256,256]{1,0:T(8,128)(2,1)} %constant.10.clone.psi2, ...), custom_call_target="tpu_custom_call" | custom-call | tf_op jit(solution)/shard_map/sky_coefficients/pallas_call | solution.py:329
  39.8 0.7 %reshape.31 = f32[8,2,1152]{2,1,0:T(2,128)} reshape(f32[16,1152]{1,0:T(8,128)S(1)} %sky_coefficients.1) | data formatting | bytes 147456 | tf_op jit(solution)/shard_map/reshape | solution.py:364

commit v6 on v5

--- a/solution.py
+++ b/solution.py
@@ -249,12 +249,13 @@
         return c
 
     lax.fori_loop(1, NG, settle_c, 0)
-    coef[...] = lax.dot_general(
+    rows = lax.dot_general(
         got_c[...].reshape(128, 128).astype(BF16), perm_v[...], (((0,), (0,)), ((), ())), preferred_element_type=F32
-    ).astype(BF16)
-    diagonal = (lax.broadcasted_iota(jnp.int32, (16, 1024), 0) >> 1) == (
-        lax.broadcasted_iota(jnp.int32, (16, 1024), 1) >> 7
-    )
+    )
+    diagonal = ((lax.broadcasted_iota(jnp.int32, (128, 1024), 0) >> 1) & 7) == (
+        lax.broadcasted_iota(jnp.int32, (128, 1024), 1) >> 7
+    )
+    coef[...] = jnp.where(diagonal, jnp.concatenate([rows] * 8, axis=1), 0.0).astype(BF16)
 
     def copy_e(e, slot):
         return pltpu.make_async_remote_copy(
@@ -269,8 +270,7 @@
     def contract(i, c):
         e = far(i, 1)
         load(e).wait()
-        rows = coef[pl.ds(pl.multiple_of(e * 16, 16), 16), :].astype(F32)
-        left = jnp.where(diagonal, jnp.concatenate([rows] * 8, axis=1), 0.0).astype(BF16)
+        left = coef[pl.ds(pl.multiple_of(e * 16, 16), 16), :]
         part = jnp.dot(left, wig[pl.ds(pl.multiple_of(e * 1024, 1024), 1024), :], preferred_element_type=F32)
 
         @pl.when(i < NB)
@@ -286,6 +286,21 @@
 
     lax.fori_loop(1, NB + 1, contract, 0)
 
+    def sent_beam(i, c):
+        e = lax.rem(beam + i, NB)
+        copy_a(e, e).wait_send()
+        copy_e(e, e).wait_send()
+        return c
+
+    def sent_blk(i, c):
+        g = lax.rem(blk + i, NG)
+        copy_s(g, g).wait_send()
+        copy_c(g, g).wait_send()
+        return c
+
+    lax.fori_loop(1, NB, sent_beam, 0)
+    lax.fori_loop(1, NG, sent_blk, 0)
+
     def settle_e(i, c):
         e = far(i, -1)
         copy_e(e, e).wait_recv()
@@ -293,21 +308,6 @@
         return c
 
     lax.fori_loop(1, NB, settle_e, 0)
-
-    def sent_beam(i, c):
-        e = lax.rem(beam + i, NB)
-        copy_a(e, e).wait_send()
-        copy_e(e, e).wait_send()
-        return c
-
-    def sent_blk(i, c):
-        g = lax.rem(blk + i, NG)
-        copy_s(g, g).wait_send()
-        copy_c(g, g).wait_send()
-        return c
-
-    lax.fori_loop(1, NB, sent_beam, 0)
-    lax.fori_loop(1, NG, sent_blk, 0)
 
 
 ANY = pl.BlockSpec(memory_space=pl.ANY)
@@ -342,7 +342,7 @@
             pltpu.VMEM((512, 128), BF16),
             pltpu.VMEM((NG, 8, 128), F32),
             pltpu.VMEM((NG, 8, 128), F32),
-            pltpu.VMEM((128, 128), BF16),
+            pltpu.VMEM((128, 1024), BF16),
             pltpu.VMEM((NB, 16, L), BF16),
             pltpu.VMEM((NB, 16, L), BF16),
             dma((11,)),

time: 40.7 us -> 40.4 us (level)
  no operation moved by 1% of the time
where the time goes in v6:
time: 40.4 us; the launch traced here: 40.3 us
  Pallas kernels  39.6 us (98%)
  local copies, waits for them, and re-layouts  0.68 us (2%)
    pallas_call x1, Pallas kernels, shards(): pl.pallas_call(kernel, out_shape=pltpu.VMEM((16, L), F32), in_specs=[ANY]...  39.6 us

profile of v6, /device:TPU:1, one launch (start us, length us, event | category | flops | bytes accessed | tf_op | source)
XLA Modules:
  0.0 40.3 jit_solution(5550071620188459973)
XLA Ops:
  0.0 39.6 %sky_coefficients.1 = f32[16,1152]{1,0:T(8,128)S(1)} custom-call(f32[128,128]{1,0:T(8,128)} %bitcast.8, f32[128,128]{1,0:T(8,128)} %bitcast.9, s32[128,128]{1,0:T(8,128)} %bitcast.10, s32[128,128]{1,0:T(8,128)} %bitcast.11, s32[128,128]{1,0:T(8,128)} %bitcast.12, s32[1,128]{1,0:T(1,128)} %bitcast.13, bf16[256,256]{1,0:T(8,128)(2,1)} %constant.10.clone.psi2, ...), custom_call_target="tpu_custom_call" | custom-call | tf_op jit(solution)/shard_map/sky_coefficients/pallas_call | solution.py:329
  39.6 0.7 %reshape.31 = f32[8,2,1152]{2,1,0:T(2,128)} reshape(f32[16,1152]{1,0:T(8,128)S(1)} %sky_coefficients.1) | data formatting | bytes 147456 | tf_op jit(solution)/shard_map/reshape | solution.py:364
